TPU v7x, 512 devices: a whole 4x8x8 slice. The times are simulated.
512 devices in a mesh: group: 16 (over y, core), dev: 32 (over x, z).
Axes of the slice: x: 4, y: 8, z: 8, core: 2. Of those that a mesh axis runs over, the one named last changes fastest.
Arguments:
- coarse_temp: float32 [128, 512, 128], P('group', 'dev'), may hold values from 0.5 to 1.5
- coarse_cond: float32 [128, 512, 128], P('group', 'dev'), may hold values from 0.25 to 1
- routes: int32 [16, 32, 8, 16, 1], P('group', 'dev'), may hold values from 0 to 31; in each aligned block of 128 rows (0 to 127, 128 to 255, ..., all dimensions but the last counted through in order) at most 6 rows name the same one
- track_start: int32 [16, 32, 8, 16], P('group', 'dev'), may hold values from 0 to 127
- track_depth: int32 [16, 32, 8, 16], P('group', 'dev'), may hold values from 2 to 64
- power: float32 [16, 32, 8, 16], P('group', 'dev'), may hold values from 0.2 to 1
- fine_temp: float32 [16, 32, 32, 6, 4, 256], P('group', 'dev'), may hold values from 0.5 to 1.5
- fine_strain: float32 [16, 32, 32, 6, 4, 256], P('group', 'dev'), may hold values from -1 to 1
Outputs:
- coarse_next: float32 [128, 512, 128], P('group', 'dev')
- fine_temp_next: float32 [16, 32, 32, 6, 4, 256], P('group', 'dev')
- fine_strain_next: float32 [16, 32, 32, 6, 4, 256], P('group', 'dev')
Inputs may be any that keep to these rules, and one draw needn't show every extreme that they name: `routes`: among the coarse columns of one device, no owner is named more than 6 times, a bound that some block reaches; every owner is named by some column of the group.
All inputs are finite; a program needn't handle non-finite values.
Results may differ from a plain program's by a relative error of at most 0.0003.
Values sent between devices are 32-bit elements; how exact they have to be, the bound alone decides.
A program may use at most 64 MiB of HBM per device.

v0:
```python
import jax
import jax.numpy as jnp
from jax import lax
from jax.sharding import PartitionSpec as P

R_COARSE = 0.08
R_FINE = 0.16
YIELD_BASE = 0.6
MELT_TEMP = 3.0
REF_TEMP = 1.0
YIELD_FLOOR = 0.05


def extended(shard, sides, width):
    for axis, dim in sides:
        count, length = (lax.axis_size(axis), shard.shape[dim])
        up = [(i, (i + 1) % count) for i in range(count - 1)]
        down = [(j, i) for i, j in up]
        last = lax.slice_in_dim(shard, length - width, length, axis=dim)
        first = lax.slice_in_dim(shard, 0, width, axis=dim)
        before = lax.ppermute(last, axis, up)
        after = lax.ppermute(first, axis, down)
        shard = jnp.concatenate([before, shard, after], axis=dim)
    return shard


def coarse_update(padded, conduct):
    zpad = jnp.pad(padded, ((0, 0), (0, 0), (1, 1)))
    center = zpad[1:-1, 1:-1, 1:-1]
    beside = zpad[2:, 1:-1, 1:-1] + zpad[:-2, 1:-1, 1:-1] + zpad[1:-1, 2:, 1:-1]
    beside = beside + zpad[1:-1, :-2, 1:-1] + zpad[1:-1, 1:-1, 2:] + zpad[1:-1, 1:-1, :-2]
    return center + R_COARSE * conduct * (beside - 6.0 * center)


def column_ghosts(old_pad, mid_pad):
    pieces = []
    for padded in (old_pad, mid_pad):
        pieces = pieces + [padded[:-2, 1:-1], padded[2:, 1:-1], padded[1:-1, :-2], padded[1:-1, 2:]]
    return jnp.stack(pieces, axis=2)


def owner_slots(owner_of, owner_count):
    one_hot = (owner_of[:, None] == jnp.arange(owner_count, dtype=jnp.int32)[None, :]).astype(
        jnp.int32
    )
    before = jnp.cumsum(one_hot, axis=0) - one_hot
    return jnp.sum(before * one_hot, axis=1)


def refine_z(values):
    return jnp.repeat(values, 2, axis=-1)


def fine_substep(thermal, strain, side_x, side_y, conduct_fine, source):
    above_cell = jnp.concatenate([thermal[..., 1:], jnp.zeros_like(thermal[..., :1])], axis=-1)
    below_cell = jnp.concatenate([jnp.zeros_like(thermal[..., :1]), thermal[..., :-1]], axis=-1)
    beside = (
        jnp.flip(thermal, -3) + jnp.flip(thermal, -2) + side_x + side_y + above_cell + below_cell
    )
    thermal = thermal + R_FINE * conduct_fine * (beside - 6.0 * thermal) + source
    stress = REF_TEMP - thermal - strain
    yield_limit = YIELD_BASE * jnp.maximum(1.0 - thermal / MELT_TEMP, YIELD_FLOOR)
    strain = strain + (stress - jnp.clip(stress, -yield_limit, yield_limit))
    return (thermal, strain)


def fine_advance(thermal, strain, ghosts, conduct, heat_rate, heat_start, heat_depth):
    depth_pos = jnp.arange(thermal.shape[-1], dtype=jnp.int32)
    inside = (depth_pos >= heat_start[..., None]) & (
        depth_pos < (heat_start + heat_depth)[..., None]
    )
    source = jnp.where(inside, heat_rate[..., None], 0.0)[..., None, None, :]
    conduct_fine = refine_z(conduct)[..., None, None, :]
    for substep in range(2):
        side = refine_z(ghosts[..., 4 * substep : 4 * substep + 4, :])
        side_x = side[..., 0:2, :][..., :, None, :]
        side_y = side[..., 2:4, :][..., None, :, :]
        thermal, strain = fine_substep(thermal, strain, side_x, side_y, conduct_fine, source)
    average = thermal.reshape(thermal.shape[:-3] + (4, thermal.shape[-1] // 2, 2)).mean(
        axis=(-3, -1)
    )
    return (thermal, strain, average)


def local(
    coarse_temp, coarse_cond, routes, track_start, track_depth, power, fine_temp, fine_strain
):
    dev_count = lax.axis_size("dev")
    block_x, block_y, depth_cells = coarse_temp.shape
    row_count = block_x * block_y
    slot_count = fine_temp.shape[3]
    fine_cells = 2 * depth_cells
    old_pad = extended(coarse_temp, (("group", 0), ("dev", 1)), 1)
    coarse_new = coarse_update(old_pad, coarse_cond)
    new_pad = extended(coarse_new, (("group", 0), ("dev", 1)), 1)
    mid_pad = 0.5 * (old_pad + new_pad)
    ghosts = column_ghosts(old_pad, mid_pad).reshape(row_count, 8, depth_cells)
    owner_of = routes.reshape(row_count)
    slot_of = owner_slots(owner_of, dev_count)
    heat_start = track_start.reshape(row_count)
    heat_depth = track_depth.reshape(row_count)
    heat_rate = power.reshape(row_count)
    cond_rows = coarse_cond.reshape(row_count, depth_cells)
    states = jnp.stack(
        [
            fine_temp.reshape(dev_count, slot_count, 4, fine_cells),
            fine_strain.reshape(dev_count, slot_count, 4, fine_cells),
        ],
        axis=2,
    )
    arrived = lax.all_to_all(states, "dev", split_axis=0, concat_axis=0, tiled=True)
    picked = arrived[owner_of, slot_of]
    thermal = picked[:, 0].reshape(row_count, 2, 2, fine_cells)
    strain = picked[:, 1].reshape(row_count, 2, 2, fine_cells)
    thermal, strain, average = fine_advance(
        thermal, strain, ghosts, cond_rows, heat_rate, heat_start, heat_depth
    )
    coarse_next = average.reshape(block_x, block_y, depth_cells)
    result = jnp.stack(
        [thermal.reshape(row_count, 4, fine_cells), strain.reshape(row_count, 4, fine_cells)],
        axis=1,
    )
    outgoing = (
        jnp.zeros((dev_count, slot_count, 2, 4, fine_cells), jnp.float32)
        .at[owner_of, slot_of]
        .set(result)
    )
    returned = lax.all_to_all(outgoing, "dev", split_axis=0, concat_axis=0, tiled=True)
    temp_next = returned[:, :, 0].reshape(fine_temp.shape)
    strain_next = returned[:, :, 1].reshape(fine_strain.shape)
    return (coarse_next, temp_next, strain_next)


def solution(mesh):
    placed = (
        P("group", "dev", None),
        P("group", "dev", None),
        P("group", "dev", None, None, None),
        P("group", "dev", None, None),
        P("group", "dev", None, None),
        P("group", "dev", None, None),
        P("group", "dev", None, None, None, None),
        P("group", "dev", None, None, None, None),
    )
    return jax.shard_map(
        local,
        mesh=mesh,
        in_specs=placed,
        out_specs=(
            P("group", "dev", None),
            P("group", "dev", None, None, None, None),
            P("group", "dev", None, None, None, None),
        ),
        check_vma=False,
    )
```

profile of v0, /device:TPU:24, one launch (start us, length us, event | category | flops | bytes accessed | tf_op | source)
XLA Modules:
  0.0 151.0 jit_solution(15434689375782028773)
XLA Ops:
  0.6 2.9 %pad_maximum_fusion = f32[32,6,2,4,256]{4,3,1,2,0:T(4,128)} fusion(f32[32,6,1,4,256]{4,3,1,2,0:T(4,128)} %bitcast.45, f32[32,6,1,4,256]{4,3,1,2,0:T(4,128)} %bitcast.46), kind=kLoop, calls=%fused_computation.2 | loop fusion | flops 393216 | bytes 3145728 | tf_op jit(solution)/shard_map/stack | solution.py:104
  3.6 13.3 %all-to-all-start = ((f32[32,6,2,4,256]{4,3,1,2,0:T(4,128)}), f32[32,6,2,4,256]{4,3,1,2,0:T(4,128)S(1)}, u32[]{:S(2)}, u32[]{:S(2)}) async-start(f32[32,6,2,4,256]{4,3,1,2,0:T(4,128)} %pad_maximum_fusion), calls=%async_computation | async-start | bytes 3145728 | tf_op jit(solution)/shard_map/all_to_all | solution.py:111
  16.9 1.9 %collective-permute-start = (f32[1,16,128]{2,1,0:T(8,128)S(1)}, f32[1,16,128]{2,1,0:T(8,128)S(1)}, u32[]{:S(2)}, u32[]{:S(2)}) collective-permute-start(f32[1,16,128]{2,1,0:T(8,128)S(1)} %get-tuple-element.39), channel_id=1, source_target_pairs={{0,32},{32,64},{64,96},{96,128},{128,160},{160,192},{192,224},{224... | collective-permute-start | bytes 24584 | tf_op jit(solution)/shard_map/ppermute | solution.py:21
  18.9 3.6 %collective-permute-start.1 = (f32[1,16,128]{2,1,0:T(8,128)S(1)}, f32[1,16,128]{2,1,0:T(8,128)S(1)}, u32[]{:S(2)}, u32[]{:S(2)}) collective-permute-start(f32[1,16,128]{2,1,0:T(8,128)S(1)} %get-tuple-element.38), channel_id=1, source_target_pairs={{32,0},{64,32},{96,64},{128,96},{160,128},{192,160},{224,192},{256... | collective-permute-start | bytes 24584 | tf_op jit(solution)/shard_map/ppermute | solution.py:22
  24.8 1.3 collective-permute-start.3
  26.1 4.5 %collective-permute-start.2 = (f32[10,1,128]{2,1,0:T(1,128)S(1)}, f32[10,1,128]{2,1,0:T(1,128)S(1)}, u32[]{:S(2)}, u32[]{:S(2)}) collective-permute-start(f32[10,1,128]{2,1,0:T(1,128)S(1)} %get-tuple-element.31), channel_id=1, source_target_pairs={{0,1},{1,2},{2,3},{3,4},{4,5},{5,6},{6,7},{7,8},{8,9},{9,10},{10,1... | collective-permute-start | bytes 15368 | tf_op jit(solution)/shard_map/ppermute | solution.py:21
  30.6 22.1 %collective-permute-done.3 = f32[10,1,128]{2,1,0:T(1,128)S(1)} collective-permute-done((f32[10,1,128]{2,1,0:T(1,128)S(1)}, f32[10,1,128]{2,1,0:T(1,128)S(1)}, u32[]{:S(2)}, u32[]{:S(2)}) %collective-permute-start.3) | collective-permute-done | bytes 5152 | tf_op jit(solution)/shard_map/ppermute | solution.py:22
  53.0 1.9 %collective-permute-start.5 = (f32[1,16,128]{2,1,0:T(8,128)S(1)}, f32[1,16,128]{2,1,0:T(8,128)S(1)}, u32[]{:S(2)}, u32[]{:S(2)}) collective-permute-start(f32[1,16,128]{2,1,0:T(8,128)S(1)} %get-tuple-element.37), channel_id=1, source_target_pairs={{32,0},{64,32},{96,64},{128,96},{160,128},{192,160},{224,192},{256... | collective-permute-start | bytes 24584 | tf_op jit(solution)/shard_map/ppermute | solution.py:22
  54.9 2.4 %collective-permute-start.4 = (f32[1,16,128]{2,1,0:T(8,128)S(1)}, f32[1,16,128]{2,1,0:T(8,128)S(1)}, u32[]{:S(2)}, u32[]{:S(2)}) collective-permute-start(f32[1,16,128]{2,1,0:T(8,128)S(1)} %get-tuple-element.36), channel_id=1, source_target_pairs={{0,32},{32,64},{64,96},{96,128},{128,160},{160,192},{192,224},{224... | collective-permute-start | bytes 24584 | tf_op jit(solution)/shard_map/ppermute | solution.py:21
  57.5 2.4 %collective-permute-done.4 = f32[1,16,128]{2,1,0:T(8,128)S(1)} collective-permute-done((f32[1,16,128]{2,1,0:T(8,128)S(1)}, f32[1,16,128]{2,1,0:T(8,128)S(1)}, u32[]{:S(2)}, u32[]{:S(2)}) %collective-permute-start.4) | collective-permute-done | bytes 8224 | tf_op jit(solution)/shard_map/ppermute | solution.py:21
  59.9 1.3 collective-permute-start.7
  61.2 4.5 %collective-permute-start.6 = (f32[10,1,128]{2,1,0:T(1,128)S(1)}, f32[10,1,128]{2,1,0:T(1,128)S(1)}, u32[]{:S(2)}, u32[]{:S(2)}) collective-permute-start(f32[10,1,128]{2,1,0:T(1,128)S(1)} %get-tuple-element.29), channel_id=1, source_target_pairs={{0,1},{1,2},{2,3},{3,4},{4,5},{5,6},{6,7},{7,8},{8,9},{9,10},{10,1... | collective-permute-start | bytes 15368 | tf_op jit(solution)/shard_map/ppermute | solution.py:21
  69.2 0.9 copy.39
  70.1 1.3 gather_fusion
  72.7 1.4 rev.15
  74.1 2.2 %add_add_fusion.1 = f32[128,2,2,256]{3,2,1,0:T(2,128)S(1)} fusion(f32[128,2,2,256]{3,2,1,0:T(2,128)S(1)} %reshape_squeeze.12, f32[128,2,2,255]{3,2,1,0:T(2,128)S(1)} %get-tuple-element.24, f32[128,2,2,255]{3,2,1,0:T(2,128)S(1)} %get-tuple-element.23, f32[128,2,2,256]{3,2,1,0:T(2,128)S(1)} %rev.15, f32[128,256]{1,0:T(8,128)S(1)} %fusion.1, ...), kind=kLoop, calls=%fused_computation.8 | loop fusion | flops 1310720 | bytes 3403776 | tf_op jit(solution)/shard_map/add | solution.py:60
  76.3 1.5 fusion.14
  77.8 1.4 rev.17
  79.6 3.5 %subtract_add_fusion = (f32[128,2,2,256]{3,2,1,0:T(2,128)S(1)}, f32[128,2,2,256]{3,2,1,0:T(2,128)S(1)}) fusion(f32[128,2,2,256]{3,2,1,0:T(2,128)S(1)} %reshape_squeeze.13, f32[128,2,2,256]{3,2,1,0:T(2,128)S(1)} %add_add_fusion.1, f32[128,256]{1,0:T(8,128)S(1)} %fusion.1, f32[128,2,2,255]{3,2,1,0:T(2,128)} %get-tuple-element.20, ...), kind=kLoop, calls=%fused_computation.6 | loop fusion | flops 4194304 | bytes 4452352 | tf_op jit(solution)/shard_map/add | solution.py:63
  84.3 1.5 %broadcast_in_dim.45 = f32[32,6,2,4,256]{4,3,2,1,0:T(4,128)} broadcast(f32[]{:T(128)} %constant.17.clone.1), dimensions={} | broadcast | bytes 1572868 | tf_op jit(solution)/shard_map/broadcast_in_dim | solution.py:124
  85.8 13.8 %scatter_fusion = f32[32,6,2,4,256]{4,3,2,1,0:T(4,128)} fusion(f32[32,6,2,4,256]{4,3,2,1,0:T(4,128)} %broadcast_in_dim.45, s32[128]{0:T(128)S(1)} %get-tuple-element.8, f32[128,2,4,256]{3,2,1,0:T(4,128)S(1)} %pad_maximum_fusion.1), kind=kCustom, calls=%fused_computation.1 | custom fusion | bytes 3146752 | tf_op jit(solution)/shard_map/scatter | solution.py:126
  99.7 11.2 %all-to-all-start.1 = ((f32[32,6,2,4,256]{4,3,2,1,0:T(4,128)}), f32[32,6,2,4,256]{4,3,2,1,0:T(4,128)S(1)}, u32[]{:S(2)}, u32[]{:S(2)}) async-start(f32[32,6,2,4,256]{4,3,2,1,0:T(4,128)} %scatter_fusion), calls=%async_computation.1 | async-start | bytes 3145728 | tf_op jit(solution)/shard_map/all_to_all | solution.py:128
  112.3 37.3 %all-to-all-done.1 = f32[32,6,2,4,256]{4,3,2,1,0:T(4,128)S(1)} async-done(((f32[32,6,2,4,256]{4,3,2,1,0:T(4,128)}), f32[32,6,2,4,256]{4,3,2,1,0:T(4,128)S(1)}, u32[]{:S(2)}, u32[]{:S(2)}) %all-to-all-start.1) | async-done | bytes 1572896 | tf_op jit(solution)/shard_map/all_to_all | solution.py:128
  149.6 1.4 slice_bitcast_fusion
  (69 shorter events, 10.1 us)
Async XLA Ops:
  3.6 13.4 %copy-start = (f32[8,16,128]{2,1,0:T(8,128)S(1)}, f32[8,16,128]{2,1,0:T(8,128)}, u32[]{:S(2)}) copy-start(f32[8,16,128]{2,1,0:T(8,128)} %param.8) | copy-start | bytes 196612
  3.6 19.0 %copy-start.2 = (s32[1,1,8,16,1]{3,4,2,1,0:T(1,128)S(1)}, s32[1,1,8,16,1]{3,4,2,1,0:T(1,128)}, u32[]{:S(2)}) copy-start(s32[1,1,8,16,1]{3,4,2,1,0:T(1,128)} %param.10) | copy-start | bytes 1540
  3.6 19.0 %copy-start.3 = (f32[1,1,8,16]{3,2,1,0:T(8,128)S(1)}, f32[1,1,8,16]{3,2,1,0:T(8,128)}, u32[]{:S(2)}) copy-start(f32[1,1,8,16]{3,2,1,0:T(8,128)} %param.13) | copy-start | bytes 1540
  3.6 19.1 %copy-start.4 = (s32[1,1,8,16]{3,2,1,0:T(8,128)S(1)}, s32[1,1,8,16]{3,2,1,0:T(8,128)}, u32[]{:S(2)}) copy-start(s32[1,1,8,16]{3,2,1,0:T(8,128)} %param.11) | copy-start | bytes 1540
  3.6 19.2 %copy-start.5 = (s32[1,1,8,16]{3,2,1,0:T(8,128)S(1)}, s32[1,1,8,16]{3,2,1,0:T(8,128)}, u32[]{:S(2)}) copy-start(s32[1,1,8,16]{3,2,1,0:T(8,128)} %param.12) | copy-start | bytes 1540
  3.6 49.2 %copy-start.1 = (f32[8,16,128]{2,1,0:T(8,128)S(1)}, f32[8,16,128]{2,1,0:T(8,128)}, u32[]{:S(2)}) copy-start(f32[8,16,128]{2,1,0:T(8,128)} %param.9) | copy-start | bytes 196612
  3.6 66.5 %all-to-all-start = ((f32[32,6,2,4,256]{4,3,1,2,0:T(4,128)}), f32[32,6,2,4,256]{4,3,1,2,0:T(4,128)S(1)}, u32[]{:S(2)}, u32[]{:S(2)}) async-start(f32[32,6,2,4,256]{4,3,1,2,0:T(4,128)} %pad_maximum_fusion), calls=%async_computation | async-start | bytes 3145728 | tf_op jit(solution)/shard_map/all_to_all | solution.py:111
  16.9 7.8 %collective-permute-start = (f32[1,16,128]{2,1,0:T(8,128)S(1)}, f32[1,16,128]{2,1,0:T(8,128)S(1)}, u32[]{:S(2)}, u32[]{:S(2)}) collective-permute-start(f32[1,16,128]{2,1,0:T(8,128)S(1)} %get-tuple-element.39), channel_id=1, source_target_pairs={{0,32},{32,64},{64,96},{96,128},{128,160},{160,192},{192,224},{224... | collective-permute-start | bytes 24584 | tf_op jit(solution)/shard_map/ppermute | solution.py:21
  18.9 5.9 %collective-permute-start.1 = (f32[1,16,128]{2,1,0:T(8,128)S(1)}, f32[1,16,128]{2,1,0:T(8,128)S(1)}, u32[]{:S(2)}, u32[]{:S(2)}) collective-permute-start(f32[1,16,128]{2,1,0:T(8,128)S(1)} %get-tuple-element.38), channel_id=1, source_target_pairs={{32,0},{64,32},{96,64},{128,96},{160,128},{192,160},{224,192},{256... | collective-permute-start | bytes 24584 | tf_op jit(solution)/shard_map/ppermute | solution.py:22
  24.8 28.0 %collective-permute-start.3 = (f32[10,1,128]{2,1,0:T(1,128)S(1)}, f32[10,1,128]{2,1,0:T(1,128)S(1)}, u32[]{:S(2)}, u32[]{:S(2)}) collective-permute-start(f32[10,1,128]{2,1,0:T(1,128)S(1)} %get-tuple-element.32), channel_id=1, source_target_pairs={{1,0},{2,1},{3,2},{4,3},{5,4},{6,5},{7,6},{8,7},{9,8},{10,9},{11,1... | collective-permute-start | bytes 15368 | tf_op jit(solution)/shard_map/ppermute | solution.py:22
  26.1 26.7 %collective-permute-start.2 = (f32[10,1,128]{2,1,0:T(1,128)S(1)}, f32[10,1,128]{2,1,0:T(1,128)S(1)}, u32[]{:S(2)}, u32[]{:S(2)}) collective-permute-start(f32[10,1,128]{2,1,0:T(1,128)S(1)} %get-tuple-element.31), channel_id=1, source_target_pairs={{0,1},{1,2},{2,3},{3,4},{4,5},{5,6},{6,7},{7,8},{8,9},{9,10},{10,1... | collective-permute-start | bytes 15368 | tf_op jit(solution)/shard_map/ppermute | solution.py:21
  53.0 4.5 %collective-permute-start.5 = (f32[1,16,128]{2,1,0:T(8,128)S(1)}, f32[1,16,128]{2,1,0:T(8,128)S(1)}, u32[]{:S(2)}, u32[]{:S(2)}) collective-permute-start(f32[1,16,128]{2,1,0:T(8,128)S(1)} %get-tuple-element.37), channel_id=1, source_target_pairs={{32,0},{64,32},{96,64},{128,96},{160,128},{192,160},{224,192},{256... | collective-permute-start | bytes 24584 | tf_op jit(solution)/shard_map/ppermute | solution.py:22
  54.9 5.0 %collective-permute-start.4 = (f32[1,16,128]{2,1,0:T(8,128)S(1)}, f32[1,16,128]{2,1,0:T(8,128)S(1)}, u32[]{:S(2)}, u32[]{:S(2)}) collective-permute-start(f32[1,16,128]{2,1,0:T(8,128)S(1)} %get-tuple-element.36), channel_id=1, source_target_pairs={{0,32},{32,64},{64,96},{96,128},{128,160},{160,192},{192,224},{224... | collective-permute-start | bytes 24584 | tf_op jit(solution)/shard_map/ppermute | solution.py:21
  59.9 8.0 %collective-permute-start.7 = (f32[10,1,128]{2,1,0:T(1,128)S(1)}, f32[10,1,128]{2,1,0:T(1,128)S(1)}, u32[]{:S(2)}, u32[]{:S(2)}) collective-permute-start(f32[10,1,128]{2,1,0:T(1,128)S(1)} %get-tuple-element.30), channel_id=1, source_target_pairs={{1,0},{2,1},{3,2},{4,3},{5,4},{6,5},{7,6},{8,7},{9,8},{10,9},{11,1... | collective-permute-start | bytes 15368 | tf_op jit(solution)/shard_map/ppermute | solution.py:22
  61.2 6.7 %collective-permute-start.6 = (f32[10,1,128]{2,1,0:T(1,128)S(1)}, f32[10,1,128]{2,1,0:T(1,128)S(1)}, u32[]{:S(2)}, u32[]{:S(2)}) collective-permute-start(f32[10,1,128]{2,1,0:T(1,128)S(1)} %get-tuple-element.29), channel_id=1, source_target_pairs={{0,1},{1,2},{2,3},{3,4},{4,5},{5,6},{6,7},{7,8},{8,9},{9,10},{10,1... | collective-permute-start | bytes 15368 | tf_op jit(solution)/shard_map/ppermute | solution.py:21
  99.7 50.0 %all-to-all-start.1 = ((f32[32,6,2,4,256]{4,3,2,1,0:T(4,128)}), f32[32,6,2,4,256]{4,3,2,1,0:T(4,128)S(1)}, u32[]{:S(2)}, u32[]{:S(2)}) async-start(f32[32,6,2,4,256]{4,3,2,1,0:T(4,128)} %scatter_fusion), calls=%async_computation.1 | async-start | bytes 3145728 | tf_op jit(solution)/shard_map/all_to_all | solution.py:128
where the time goes:
time: 152 us; the launch traced here: 151 us
  waiting for transfers between devices  61.9 us (41%)
  starting transfers between devices  46 us (30%)
  local copies, waits for them, and re-layouts  31.1 us (20%)
  other arithmetic  10.9 us (7%)
    all_to_all x1, waiting for transfers between devices, local(): lax.all_to_all(outgoing, 'dev', split_axis=0, concat_axis=0, tiled=True)  37.3 us
    ppermute x4, waiting for transfers between devices, extended(): after = lax.ppermute(first, axis, down)  22.2 us
    scatter x1, local copies, waits for them, and re-layouts, local(): outgoing = jnp.zeros((dev_count, slot_count, 2, 4, fine_cells), jnp.float...  13.8 us
    ppermute x4, starting transfers between devices, extended(): before = lax.ppermute(last, axis, up)  13.4 us
    all_to_all x1, starting transfers between devices, local(): lax.all_to_all(states, 'dev', split_axis=0, concat_axis=0, tiled=True)  13.3 us
    all_to_all x1, starting transfers between devices, local(): lax.all_to_all(outgoing, 'dev', split_axis=0, concat_axis=0, tiled=True)  11.2 us
    ppermute x4, starting transfers between devices, extended(): after = lax.ppermute(first, axis, down)  8.15 us
    add x1, other arithmetic, fine_substep(): strain = strain + (stress - jnp.clip(stress, -yield_limit, yield_limit))  3.52 us
  transfers between devices with their start and end apart: 10, of which 3 were waited for; matrix products, arithmetic and copies ran while one was open for 5% of the time, Pallas kernels for 0%

commit v1 on v0

v1 whole, which is shorter than its diff:
```python
import functools

import jax
import jax.numpy as jnp
from jax import lax
from jax.experimental import pallas as pl
from jax.experimental.pallas import tpu as pltpu
from jax.sharding import PartitionSpec as P

R_COARSE = 0.08
R_FINE = 0.16
YIELD_BASE = 0.6
MELT_TEMP = 3.0
YIELD_FLOOR = 0.05

MESH = pl.DeviceIdType.MESH
F32 = jnp.float32
BF16 = jnp.bfloat16

X_CHIPS, Z_CHIPS = 4, 8
DEVS = X_CHIPS * Z_CHIPS
SLOTS = 6
COLS = DEVS * SLOTS
BX, BY, NZ = 8, 16, 128
ROWS = BX * BY

MEAN_AT = 0
COND_AT = 12
SCAL_AT = 18
GHOST_AT = 20
FIRST = 16
MSG = 56

CORNERS = ((1, 1), (1, -1), (-1, 1), (-1, -1))


def offset_of(step):
    pair = step // X_CHIPS
    return step % X_CHIPS, ((pair + 1) // 2) * (2 * (pair % 2) - 1)


def split(value):
    high = value.astype(BF16)
    return high, (value - high.astype(F32)).astype(BF16)


def pick(chooser, value, dims=((1,), (0,))):
    total = None
    for part in split(value):
        term = lax.dot_general(chooser, part, (dims, ((), ())), preferred_element_type=F32)
        total = term if total is None else total + term
    return total


def iota(shape, dim):
    return lax.broadcasted_iota(jnp.int32, shape, dim)


def kernel(
    par, ct, cc, ft, fs, cnew, tout, sout,
    outb, land, hys, hyl, hxs, hxl, hcs, hcl, oe, ce, me, field, side,
    hsend, hrecv, asend, arecv, bsend, brecv, lsem,
):
    group = lax.axis_index("group")
    groups = lax.axis_size("group")
    dev = lax.axis_index("dev")
    dx, dz = dev // Z_CHIPS, dev % Z_CHIPS

    def target(step):
        ox, oz = offset_of(step)
        return ((dx + ox) % X_CHIPS) * Z_CHIPS + (dz + oz + Z_CHIPS) % Z_CHIPS

    def origin(step):
        ox, oz = offset_of(step)
        return ((dx - ox + X_CHIPS) % X_CHIPS) * Z_CHIPS + (dz - oz + Z_CHIPS) % Z_CHIPS

    def near(dg, dd):
        return {"group": (group + dg + groups) % groups, "dev": (dev + dd + DEVS) % DEVS}

    barrier = pltpu.get_barrier_semaphore()

    def greet(step, carry):
        pl.semaphore_signal(barrier, inc=1, device_id={"dev": target(step)}, device_id_type=MESH)
        return carry

    lax.fori_loop(1, DEVS, greet, 0)
    for dg, dd in ((1, 0), (-1, 0)) + CORNERS:
        pl.semaphore_signal(barrier, inc=1, device_id=near(dg, dd), device_id_type=MESH)

    for x in range(BX):
        hys[0, 2 * x:2 * x + 2] = ct[x, BY - 2:BY]
        hys[0, 16 + x:17 + x] = cc[x, BY - 1:BY]
        hys[1, 2 * x:2 * x + 2] = ct[x, 0:2]
        hys[1, 16 + x:17 + x] = cc[x, 0:1]
    for i, (lo, edge) in enumerate(((BX - 2, BX - 1), (0, 0))):
        hxs[i, 0:16] = ct[lo]
        hxs[i, 16:32] = ct[lo + 1]
        hxs[i, 32:48] = cc[edge]
    for i, (dg, dd) in enumerate(CORNERS):
        row = BX - 1 if dg > 0 else 0
        hcs[i] = jnp.broadcast_to(ct[row, BY - 1:BY] if dd > 0 else ct[row, 0:1], (8, NZ))

    power, start, depth, owner = (par[i:i + 1] for i in range(4))
    owner_b = jnp.broadcast_to(owner, (DEVS, ROWS))
    hot = jnp.where(owner_b == iota((DEVS, ROWS), 0).astype(F32), 1.0, 0.0)
    earlier = jnp.where(iota((ROWS, ROWS), 0) < iota((ROWS, ROWS), 1), 1.0, 0.0).astype(BF16)
    before = lax.dot_general(hot.astype(BF16), earlier, (((1,), (0,)), ((), ())), preferred_element_type=F32)
    slot = jnp.sum(before * hot, axis=0, keepdims=True)
    code = slot * DEVS + owner
    to_slot = jnp.where(jnp.broadcast_to(code, (COLS, ROWS)) == iota((COLS, ROWS), 0).astype(F32), 1.0, 0.0).astype(BF16)
    code_t = jnp.transpose(jnp.broadcast_to(code, (ROWS, ROWS)))
    start_t = jnp.transpose(jnp.broadcast_to(start, (ROWS, ROWS)))
    depth_t = jnp.transpose(jnp.broadcast_to(depth, (ROWS, ROWS)))
    power_t = jnp.transpose(jnp.broadcast_to(power, (ROWS, ROWS)))
    lanes = iota((ROWS, ROWS), 1).astype(F32)
    from_slot = jnp.concatenate(
        [jnp.where(code_t == lanes, 1.0, 0.0), jnp.where(code_t == lanes + ROWS, 1.0, 0.0)], axis=1
    ).astype(BF16)

    conds = pick(to_slot, cc[...].reshape(ROWS, NZ))
    for k in range(SLOTS):
        outb[pl.ds(COND_AT + k, DEVS, stride=MSG), :] = conds[k * DEVS:(k + 1) * DEVS]
    at_slot = jnp.broadcast_to(slot, (8, ROWS)) == iota((8, ROWS), 0).astype(F32)
    blocks = [jnp.where(at_slot, jnp.broadcast_to(v, (8, ROWS)), 0.0) for v in (power, start, depth)]
    blocks = blocks + [jnp.where(at_slot, 1.0, 0.0), jnp.zeros((NZ - 32, ROWS), F32)]
    scalars = pick(hot.astype(BF16), jnp.concatenate(blocks, axis=0), ((1,), (1,)))
    outb[pl.ds(SCAL_AT, DEVS, stride=MSG), :] = scalars
    outb[pl.ds(SCAL_AT + 1, DEVS, stride=MSG), :] = jnp.zeros_like(scalars)

    for k in range(SLOTS):
        for half in range(2):
            total = None
            for ab in range(4):
                term = ft[pl.ds(8 * k + 4 * half + ab, DEVS, stride=8 * SLOTS), :]
                total = term if total is None else total + term
            outb[pl.ds(MEAN_AT + SLOTS * half + k, DEVS, stride=MSG), :] = 0.25 * total

    oe[...] = jnp.zeros_like(oe)
    ce[...] = jnp.zeros_like(ce)
    for x in range(BX):
        oe[2 + x, 8:24] = ct[x]
        ce[1 + x, 8:24] = cc[x]

    def own(lo, n):
        src = outb.at[pl.ds(pl.multiple_of(dev * MSG + lo, 8), n)]
        return pltpu.make_async_copy(src, land.at[dev, pl.ds(lo, n)], lsem)

    def message(peer, sender, lo, n, send, recv):
        src = outb.at[pl.ds(pl.multiple_of(peer * MSG + lo, 8), n)]
        return pltpu.make_async_remote_copy(
            src, land.at[sender, pl.ds(lo, n)], send.at[peer], recv.at[sender],
            device_id={"dev": peer}, device_id_type=MESH,
        )

    pl.semaphore_wait(barrier, DEVS - 1 + 2 + len(CORNERS))

    halos = []
    plan = [(hys, hyl, 0, 0, 1), (hys, hyl, 1, 0, -1), (hxs, hxl, 0, 1, 0), (hxs, hxl, 1, -1, 0)]
    plan = plan + [(hcs, hcl, i, dg, dd) for i, (dg, dd) in enumerate(CORNERS)]
    for number, (src, dst, i, dg, dd) in enumerate(plan):
        copy = pltpu.make_async_remote_copy(
            src.at[i], dst.at[i], hsend.at[number], hrecv.at[number],
            device_id=near(dg, dd), device_id_type=MESH,
        )
        copy.start()
        halos.append(copy)

    def send_first(step, carry):
        message(target(step), dev, 0, FIRST, asend, arecv).start()
        return carry

    lax.fori_loop(1, DEVS, send_first, 0)
    own_first = own(0, FIRST)
    own_first.start()

    for copy in halos:
        copy.wait_recv()

    low_x, high_x = group > 0, group < groups - 1
    low_y, high_y = dev > 0, dev < DEVS - 1

    def inside(ok, value):
        return jnp.where(ok, value, 0.0)

    for x in range(BX):
        oe[2 + x, 6:8] = inside(low_y, hyl[0, 2 * x:2 * x + 2])
        oe[2 + x, 24:26] = inside(high_y, hyl[1, 2 * x:2 * x + 2])
        ce[1 + x, 7:8] = inside(low_y, hyl[0, 16 + x:17 + x])
        ce[1 + x, 24:25] = inside(high_y, hyl[1, 16 + x:17 + x])
    oe[0, 8:24] = inside(low_x, hxl[0, 0:16])
    oe[1, 8:24] = inside(low_x, hxl[0, 16:32])
    ce[0, 8:24] = inside(low_x, hxl[0, 32:48])
    oe[BX + 2, 8:24] = inside(high_x, hxl[1, 0:16])
    oe[BX + 3, 8:24] = inside(high_x, hxl[1, 16:32])
    ce[BX + 1, 8:24] = inside(high_x, hxl[1, 32:48])
    oe[1, 7:8] = inside(low_x & low_y, hcl[0, 0:1])
    oe[1, 24:25] = inside(low_x & high_y, hcl[1, 0:1])
    oe[BX + 2, 7:8] = inside(high_x & low_y, hcl[2, 0:1])
    oe[BX + 2, 24:25] = inside(high_x & high_y, hcl[3, 0:1])

    lane = iota((32, NZ), 1)
    for x in range(BX + 2):
        cur = oe[x + 1]
        beside = oe[x] + oe[x + 2] + pltpu.roll(cur, 1, 0) + pltpu.roll(cur, 31, 0)
        beside = beside + jnp.where(lane == 0, 0.0, pltpu.roll(cur, 1, 1))
        beside = beside + jnp.where(lane == NZ - 1, 0.0, pltpu.roll(cur, NZ - 1, 1))
        new = cur + R_COARSE * ce[x] * (beside - 6.0 * cur)
        me[x] = 0.5 * (cur + new)

    for x in range(BX):
        for step, (arr, at) in enumerate(((oe, x + 2), (me, x + 1))):
            west, east = arr[at - 1, 8:24], arr[at + 1, 8:24]
            south, north = arr[at, 7:23], arr[at, 9:25]
            base, along_x, along_y = west + south, east - west, north - south
            for i, value in enumerate((base, along_x, along_y)):
                f = 3 * step + i
                field[x * BY:(x + 1) * BY, f * NZ:(f + 1) * NZ] = value
            side[step, x * BY:(x + 1) * BY] = base + 0.5 * (along_x + along_y)

    ghosts = pick(to_slot, field[...])
    for f in range(6):
        for k in range(SLOTS):
            outb[pl.ds(GHOST_AT + SLOTS * f + k, DEVS, stride=MSG), :] = ghosts[k * DEVS:(k + 1) * DEVS, f * NZ:(f + 1) * NZ]

    def send_rest(step, carry):
        message(target(step), dev, FIRST, MSG - FIRST, bsend, brecv).start()
        return carry

    lax.fori_loop(1, DEVS, send_rest, 0)
    own_first.wait()
    own_rest = own(FIRST, MSG - FIRST)
    own_rest.start()

    def take_first(step, carry):
        message(origin(step), origin(step), 0, FIRST, asend, arecv).wait_recv()
        return carry

    lax.fori_loop(1, DEVS, take_first, 0)
    halves = []
    for half in range(2):
        rows = [land[:, MEAN_AT + SLOTS * half + k, :] for k in range(SLOTS)] + [jnp.zeros((2 * ROWS - COLS, NZ), F32)]
        halves.append(jnp.concatenate(rows, axis=0))
    fine = pick(from_slot, jnp.concatenate(halves, axis=1))
    row_i, col_i = iota((2 * NZ, 2 * NZ), 0), iota((2 * NZ, 2 * NZ), 1)
    wanted = jnp.where(col_i < NZ, 2 * col_i, 2 * (col_i - NZ) + 1)
    high, low = split(fine)
    apart = jnp.where(row_i == wanted, 1.0, 0.0).astype(BF16)
    dims = (((1,), (0,)), ((), ()))
    both = lax.dot_general(high, apart, dims, preferred_element_type=F32)
    both = both + lax.dot_general(low, apart, dims, preferred_element_type=F32)
    even, odd = both[:, :NZ], both[:, NZ:]
    rate = R_FINE * cc[...].reshape(ROWS, NZ)
    place = iota((ROWS, NZ), 1)

    def heat(fine_cell):
        cell = fine_cell.astype(F32)
        return jnp.where((cell >= start_t) & (cell < start_t + depth_t), power_t, 0.0)

    heat_even, heat_odd = heat(2 * place), heat(2 * place + 1)
    for step in range(2):
        under = jnp.where(place == 0, 0.0, pltpu.roll(odd, 1, 1))
        over = jnp.where(place == NZ - 1, 0.0, pltpu.roll(even, NZ - 1, 1))
        ghost = side[step]
        even, odd = (
            even + rate * (ghost + odd + under - 4.0 * even) + heat_even,
            odd + rate * (ghost + even + over - 4.0 * odd) + heat_odd,
        )
    cnew[...] = (0.5 * (even + odd)).reshape(BX, BY, NZ)

    spread = jnp.where(iota((NZ, 2 * NZ), 1) // 2 == iota((NZ, 2 * NZ), 0), 1.0, 0.0).astype(BF16)
    cell = iota((SLOTS, 2 * NZ), 1)
    cell_f = cell.astype(F32)
    dims = (((1,), (0,)), ((), ()))

    def advance(peer):
        got = land[peer]
        high, low = split(got)
        wide = lax.dot_general(high, spread, dims, preferred_element_type=F32)
        wide = wide + lax.dot_general(low, spread, dims, preferred_element_type=F32)
        rate = R_FINE * wide[COND_AT:COND_AT + SLOTS]
        row = jnp.broadcast_to(got[SCAL_AT:SCAL_AT + 1], (SLOTS, NZ))
        at, of = iota((SLOTS, NZ), 1), iota((SLOTS, NZ), 0)

        def scalar(i):
            return jnp.sum(jnp.where(at == of + 8 * i, row, 0.0), axis=1, keepdims=True)

        power, start, depth, named = (scalar(i) for i in range(4))
        source = jnp.where((cell_f >= start) & (cell_f < start + depth), power, 0.0)
        named = jnp.broadcast_to(named, (SLOTS, NZ)) > 0.5
        base_row = peer * (8 * SLOTS)

        def read(ref, ab):
            return jnp.concatenate(
                [ref[pl.ds(base_row + 4 * half + ab, SLOTS, stride=8), :] for half in range(2)], axis=1
            )

        temp = [read(ft, ab) for ab in range(4)]
        strain = [read(fs, ab) for ab in range(4)]
        for step in range(2):
            at = GHOST_AT + 3 * SLOTS * step
            base, along_x, along_y = (wide[at + SLOTS * i:at + SLOTS * (i + 1)] for i in range(3))
            ghosts = (base, base + along_y, base + along_x, base + along_x + along_y)
            after = []
            for ab in range(4):
                mine = temp[ab]
                beside = temp[ab ^ 2] + temp[ab ^ 1] + ghosts[ab]
                beside = beside + jnp.where(cell == 0, 0.0, pltpu.roll(mine, 1, 1))
                beside = beside + jnp.where(cell == 2 * NZ - 1, 0.0, pltpu.roll(mine, 2 * NZ - 1, 1))
                after.append(mine + rate * (beside - 6.0 * mine) + source)
            temp = after
            for ab in range(4):
                stress = (1.0 - temp[ab]) - strain[ab]
                limit = YIELD_BASE * jnp.maximum(1.0 - temp[ab] * (1.0 / MELT_TEMP), YIELD_FLOOR)
                strain[ab] = strain[ab] + (stress - jnp.clip(stress, -limit, limit))
        for ab in range(4):
            for half in range(2):
                rows = pl.ds(base_row + 4 * half + ab, SLOTS, stride=8)
                tout[rows, :] = jnp.where(named, temp[ab][:, half * NZ:(half + 1) * NZ], 0.0)
                sout[rows, :] = jnp.where(named, strain[ab][:, half * NZ:(half + 1) * NZ], 0.0)

    own_rest.wait()
    advance(dev)

    def take_rest(step, carry):
        peer = origin(step)
        message(peer, peer, FIRST, MSG - FIRST, bsend, brecv).wait_recv()
        advance(peer)
        return carry

    lax.fori_loop(1, DEVS, take_rest, 0)

    def sent(step, carry):
        peer = target(step)
        message(peer, dev, 0, FIRST, asend, arecv).wait_send()
        message(peer, dev, FIRST, MSG - FIRST, bsend, brecv).wait_send()
        return carry

    lax.fori_loop(1, DEVS, sent, 0)
    for copy in halos:
        copy.wait_send()


def to_tiles(fine):
    return fine.reshape(COLS, 4, 2, NZ).transpose(0, 2, 1, 3).reshape(COLS * 8, NZ)


def from_tiles(tiles, shape):
    return tiles.reshape(COLS, 2, 4, NZ).transpose(0, 2, 1, 3).reshape(shape)


def local(coarse_temp, coarse_cond, routes, track_start, track_depth, power, fine_temp, fine_strain):
    par = jnp.stack(
        [v.reshape(ROWS).astype(F32) for v in (power, track_start, track_depth, routes)]
        + [jnp.zeros((ROWS,), F32)] * 4
    )
    vmem = pl.BlockSpec(memory_space=pltpu.VMEM)
    dma = pltpu.SemaphoreType.DMA
    cnew, tout, sout = pl.pallas_call(
        kernel,
        out_shape=(
            jax.ShapeDtypeStruct((BX, BY, NZ), F32),
            jax.ShapeDtypeStruct((COLS * 8, NZ), F32),
            jax.ShapeDtypeStruct((COLS * 8, NZ), F32),
        ),
        in_specs=[vmem] * 5,
        out_specs=(vmem,) * 3,
        scratch_shapes=[
            pltpu.VMEM((DEVS * MSG, NZ), F32),
            pltpu.VMEM((DEVS, MSG, NZ), F32),
            pltpu.VMEM((2, 24, NZ), F32),
            pltpu.VMEM((2, 24, NZ), F32),
            pltpu.VMEM((2, 48, NZ), F32),
            pltpu.VMEM((2, 48, NZ), F32),
            pltpu.VMEM((4, 8, NZ), F32),
            pltpu.VMEM((4, 8, NZ), F32),
            pltpu.VMEM((BX + 4, 32, NZ), F32),
            pltpu.VMEM((BX + 2, 32, NZ), F32),
            pltpu.VMEM((BX + 2, 32, NZ), F32),
            pltpu.VMEM((ROWS, 6 * NZ), F32),
            pltpu.VMEM((2, ROWS, NZ), F32),
            dma((8,)),
            dma((8,)),
            dma((DEVS,)),
            dma((DEVS,)),
            dma((DEVS,)),
            dma((DEVS,)),
            dma,
        ],
        compiler_params=pltpu.CompilerParams(
            collective_id=1, has_side_effects=True, vmem_limit_bytes=40 * 2**20
        ),
        name="amr_step",
    )(par, coarse_temp, coarse_cond, to_tiles(fine_temp), to_tiles(fine_strain))
    return cnew, from_tiles(tout, fine_temp.shape), from_tiles(sout, fine_strain.shape)


def solution(mesh):
    placed = (
        P("group", "dev", None),
        P("group", "dev", None),
        P("group", "dev", None, None, None),
        P("group", "dev", None, None),
        P("group", "dev", None, None),
        P("group", "dev", None, None),
        P("group", "dev", None, None, None, None),
        P("group", "dev", None, None, None, None),
    )
    return jax.shard_map(
        local,
        mesh=mesh,
        in_specs=placed,
        out_specs=(
            P("group", "dev", None),
            P("group", "dev", None, None, None, None),
            P("group", "dev", None, None, None, None),
        ),
        check_vma=False,
    )
```

time: 152 us -> 51.1 us (0.34)
  the two profiles are of different devices: /device:TPU:24 before, /device:TPU:92 now
where the time goes in v1:
time: 51.1 us; the launch traced here: 50.7 us
  Pallas kernels  41.4 us (81%)
  local copies, waits for them, and re-layouts  8.58 us (17%)
  between operations  0.68 us (1%)
    pallas_call x1, Pallas kernels, local(): pl.pallas_call(kernel, out_shape=(jax.ShapeDtypeStruct((BX, BY, NZ), F32)...  41.4 us
    unnamed x17, local copies, waits for them, and re-layouts  7.54 us

profile of v1, /device:TPU:92, one launch (start us, length us, event | category | flops | bytes accessed | tf_op | source)
XLA Modules:
  0.0 50.7 jit_solution(8304571017742538266)
XLA Ops:
  0.6 0.0 copy-start.4
  0.6 0.8 %stack_reshape.3 = f32[1,128]{1,0:T(1,128)S(1)} reshape(f32[1,1,8,16]{3,2,1,0:T(8,128)} %param.13) | data formatting | bytes 1024 | tf_op jit(solution)/shard_map/stack;reshape | solution.py:352
  1.4 0.0 copy-done.4
  1.4 0.0 copy-start.5
  1.4 0.1 convert_element_type.44
  1.5 0.6 %copy-done.5 = s32[1,1,8,16]{3,2,1,0:T(8,128)S(1)} copy-done((s32[1,1,8,16]{3,2,1,0:T(8,128)S(1)}, s32[1,1,8,16]{3,2,1,0:T(8,128)}, u32[]{:S(2)}) %copy-start.5) | copy-done | bytes 536
  2.1 0.0 copy-start.6
  2.1 0.1 convert_element_type.40
  2.2 0.6 %copy-done.6 = s32[1,1,8,16]{3,2,1,0:T(8,128)S(1)} copy-done((s32[1,1,8,16]{3,2,1,0:T(8,128)S(1)}, s32[1,1,8,16]{3,2,1,0:T(8,128)}, u32[]{:S(2)}) %copy-start.6) | copy-done | bytes 536
  2.8 0.1 convert_element_type.42
  2.9 0.0 copy-start
  2.9 1.1 %copy-done = f32[1,1,32,6,4,256]{5,4,3,2,1,0:T(4,128)S(1)} copy-done((f32[1,1,32,6,4,256]{5,4,3,2,1,0:T(4,128)S(1)}, f32[1,1,32,6,4,256]{5,4,3,2,1,0:T(4,128)}, u32[]{:S(2)}) %copy-start) | copy-done | bytes 786456
  4.1 0.0 copy-start.1
  4.1 1.1 %copy-done.1 = f32[1,1,32,6,4,256]{5,4,3,2,1,0:T(4,128)S(1)} copy-done((f32[1,1,32,6,4,256]{5,4,3,2,1,0:T(4,128)S(1)}, f32[1,1,32,6,4,256]{5,4,3,2,1,0:T(4,128)}, u32[]{:S(2)}) %copy-start.1) | copy-done | bytes 786456
  5.2 0.0 copy-start.2
  5.2 0.8 %copy-done.2 = f32[8,16,128]{2,1,0:T(8,128)S(1)} copy-done((f32[8,16,128]{2,1,0:T(8,128)S(1)}, f32[8,16,128]{2,1,0:T(8,128)}, u32[]{:S(2)}) %copy-start.2) | copy-done | bytes 65560
  6.0 0.0 copy-start.3
  6.0 0.8 %copy-done.3 = f32[8,16,128]{2,1,0:T(8,128)S(1)} copy-done((f32[8,16,128]{2,1,0:T(8,128)S(1)}, f32[8,16,128]{2,1,0:T(8,128)}, u32[]{:S(2)}) %copy-start.3) | copy-done | bytes 65560
  6.9 41.4 %amr_step.1 = (f32[8,16,128]{2,1,0:T(8,128)S(1)}, f32[1536,128]{1,0:T(8,128)S(1)}, f32[1536,128]{1,0:T(8,128)S(1)}) custom-call(f32[8,128]{1,0:T(8,128)S(1)} %stack.10.par, f32[8,16,128]{2,1,0:T(8,128)S(1)} %copy-done.2, f32[8,16,128]{2,1,0:T(8,128)S(1)} %copy-done.3, f32[1536,128]{1,0:T(8,128)S(1)} %bitcast.28, f32[1536,128]{1,0:T(8,128)S(1)} %bitcast.29), custom_call_target="tpu_custom_call" | custom-call | tf_op jit(solution)/shard_map/amr_step/pallas_call | solution.py:358
  48.3 0.6 %copy.18 = f32[8,16,128]{2,1,0:T(8,128)} copy(f32[8,16,128]{2,1,0:T(8,128)S(1)} %get-tuple-element.12) | data formatting | bytes 131072
  49.0 0.9 %copy.19 = f32[1,1,32,6,4,256]{5,4,3,2,1,0:T(4,128)} copy(f32[1,1,32,6,4,256]{5,4,3,2,1,0:T(4,128)S(1)} %bitcast.27) | data formatting | bytes 1572864
  49.8 0.9 %copy.20 = f32[1,1,32,6,4,256]{5,4,3,2,1,0:T(4,128)} copy(f32[1,1,32,6,4,256]{5,4,3,2,1,0:T(4,128)S(1)} %bitcast.26) | data formatting | bytes 1572864
  (5 shorter events, 0.0 us)
Async XLA Ops:
  0.6 0.8 %copy-start.4 = (s32[1,1,8,16,1]{3,4,2,1,0:T(1,128)S(1)}, s32[1,1,8,16,1]{3,4,2,1,0:T(1,128)}, u32[]{:S(2)}) copy-start(s32[1,1,8,16,1]{3,4,2,1,0:T(1,128)} %param.10) | copy-start | bytes 1540
  1.4 0.7 %copy-start.5 = (s32[1,1,8,16]{3,2,1,0:T(8,128)S(1)}, s32[1,1,8,16]{3,2,1,0:T(8,128)}, u32[]{:S(2)}) copy-start(s32[1,1,8,16]{3,2,1,0:T(8,128)} %param.11) | copy-start | bytes 1540
  2.1 0.7 %copy-start.6 = (s32[1,1,8,16]{3,2,1,0:T(8,128)S(1)}, s32[1,1,8,16]{3,2,1,0:T(8,128)}, u32[]{:S(2)}) copy-start(s32[1,1,8,16]{3,2,1,0:T(8,128)} %param.12) | copy-start | bytes 1540
  2.9 1.1 %copy-start = (f32[1,1,32,6,4,256]{5,4,3,2,1,0:T(4,128)S(1)}, f32[1,1,32,6,4,256]{5,4,3,2,1,0:T(4,128)}, u32[]{:S(2)}) copy-start(f32[1,1,32,6,4,256]{5,4,3,2,1,0:T(4,128)} %param.14) | copy-start | bytes 2359300
  4.1 1.1 %copy-start.1 = (f32[1,1,32,6,4,256]{5,4,3,2,1,0:T(4,128)S(1)}, f32[1,1,32,6,4,256]{5,4,3,2,1,0:T(4,128)}, u32[]{:S(2)}) copy-start(f32[1,1,32,6,4,256]{5,4,3,2,1,0:T(4,128)} %param.15) | copy-start | bytes 2359300
  5.2 0.8 %copy-start.2 = (f32[8,16,128]{2,1,0:T(8,128)S(1)}, f32[8,16,128]{2,1,0:T(8,128)}, u32[]{:S(2)}) copy-start(f32[8,16,128]{2,1,0:T(8,128)} %ct.1) | copy-start | bytes 196612
  6.0 0.8 %copy-start.3 = (f32[8,16,128]{2,1,0:T(8,128)S(1)}, f32[8,16,128]{2,1,0:T(8,128)}, u32[]{:S(2)}) copy-start(f32[8,16,128]{2,1,0:T(8,128)} %cc.1) | copy-start | bytes 196612

commit v2 on v1

--- a/solution.py
+++ b/solution.py
@@ -14,6 +14,7 @@
 YIELD_FLOOR = 0.05
 
 MESH = pl.DeviceIdType.MESH
+VMEM_BYTES = 40 * 2**20
 F32 = jnp.float32
 BF16 = jnp.bfloat16
 
@@ -35,8 +36,15 @@
 
 
 def offset_of(step):
-    pair = step // X_CHIPS
-    return step % X_CHIPS, ((pair + 1) // 2) * (2 * (pair % 2) - 1)
+    away = (step + X_CHIPS) // (2 * X_CHIPS)
+    turn = (step + X_CHIPS) % (2 * X_CHIPS)
+    middle = (away == 0) | (away == Z_CHIPS // 2)
+    ox = jnp.where(middle, step % X_CHIPS, turn // 2)
+    return ox, jnp.where(middle, away, away * (1 - 2 * (turn % 2)))
+
+
+def turn_of(z):
+    return jnp.where(z < 6, z, 13 - z)
 
 
 def split(value):
@@ -57,9 +65,9 @@
 
 
 def kernel(
-    par, ct, cc, ft, fs, cnew, tout, sout,
-    outb, land, hys, hyl, hxs, hxl, hcs, hcl, oe, ce, me, field, side,
-    hsend, hrecv, asend, arecv, bsend, brecv, lsem,
+    power_in, start_in, depth_in, routes_in, ct_in, cc_in, ft_in, fs_in, cnew, tout, sout,
+        power_v, start_v, depth_v, routes_v, ct, cc, ft, fs, outb, land, hys, hyl, hxs, hxl, hcs, hcl, oe, ce, me, field, side,
+    hsend, hrecv, asend, arecv, bsend, brecv, lsem, isem,
 ):
     group = lax.axis_index("group")
     groups = lax.axis_size("group")
@@ -86,6 +94,16 @@
     lax.fori_loop(1, DEVS, greet, 0)
     for dg, dd in ((1, 0), (-1, 0)) + CORNERS:
         pl.semaphore_signal(barrier, inc=1, device_id=near(dg, dd), device_id_type=MESH)
+
+    loads = []
+    arrays = ((routes_in, routes_v), (power_in, power_v), (start_in, start_v), (depth_in, depth_v))
+    arrays = arrays + ((ct_in, ct), (cc_in, cc), (ft_in, ft), (fs_in, fs))
+    for i, (src, dst) in enumerate(arrays):
+        load = pltpu.make_async_copy(src, dst, isem.at[i])
+        load.start()
+        loads.append(load)
+    for load in loads[:6]:
+        load.wait()
 
     for x in range(BX):
         hys[0, 2 * x:2 * x + 2] = ct[x, BY - 2:BY]
@@ -100,7 +118,16 @@
         row = BX - 1 if dg > 0 else 0
         hcs[i] = jnp.broadcast_to(ct[row, BY - 1:BY] if dd > 0 else ct[row, 0:1], (8, NZ))
 
-    power, start, depth, owner = (par[i:i + 1] for i in range(4))
+    held = [power_v[...], start_v[...].astype(F32), depth_v[...].astype(F32), routes_v[:, 0, :].astype(F32)]
+    same_y = jnp.where(iota((BY, ROWS), 1) % BY == iota((BY, ROWS), 0), 1.0, 0.0).astype(BF16)
+    dims = (((1,), (0,)), ((), ()))
+    flat = None
+    for part in split(jnp.concatenate(held, axis=0)):
+        term = lax.dot_general(part, same_y, dims, preferred_element_type=F32)
+        flat = term if flat is None else flat + term
+    same_x = iota((4 * BX, ROWS), 1) // BY == iota((4 * BX, ROWS), 0) % BX
+    flat = jnp.where(same_x, flat, 0.0)
+    power, start, depth, owner = (jnp.sum(flat[BX * i:BX * (i + 1)], axis=0, keepdims=True) for i in range(4))
     owner_b = jnp.broadcast_to(owner, (DEVS, ROWS))
     hot = jnp.where(owner_b == iota((DEVS, ROWS), 0).astype(F32), 1.0, 0.0)
     earlier = jnp.where(iota((ROWS, ROWS), 0) < iota((ROWS, ROWS), 1), 1.0, 0.0).astype(BF16)
@@ -127,6 +154,7 @@
     outb[pl.ds(SCAL_AT, DEVS, stride=MSG), :] = scalars
     outb[pl.ds(SCAL_AT + 1, DEVS, stride=MSG), :] = jnp.zeros_like(scalars)
 
+    loads[6].wait()
     for k in range(SLOTS):
         for half in range(2):
             total = None
@@ -226,7 +254,16 @@
         message(target(step), dev, FIRST, MSG - FIRST, bsend, brecv).start()
         return carry
 
-    lax.fori_loop(1, DEVS, send_rest, 0)
+    def by_turn(i, carry):
+        peer = (dx + i) % X_CHIPS * Z_CHIPS + turn_of(i // X_CHIPS)
+
+        @pl.when(peer != dev)
+        def _():
+            message(peer, dev, FIRST, MSG - FIRST, bsend, brecv).start()
+
+        return carry
+
+    lax.fori_loop(0, DEVS, by_turn, 0)
     own_first.wait()
     own_rest = own(FIRST, MSG - FIRST)
     own_rest.start()
@@ -319,15 +356,22 @@
                 sout[rows, :] = jnp.where(named, strain[ab][:, half * NZ:(half + 1) * NZ], 0.0)
 
     own_rest.wait()
-    advance(dev)
-
-    def take_rest(step, carry):
-        peer = origin(step)
-        message(peer, peer, FIRST, MSG - FIRST, bsend, brecv).wait_recv()
-        advance(peer)
-        return carry
-
-    lax.fori_loop(1, DEVS, take_rest, 0)
+    loads[7].wait()
+
+    def take_rest(turn, carry):
+        for i in range(X_CHIPS):
+            step = turn * X_CHIPS + i
+
+            @pl.when(step > 0)
+            def _():
+                peer = origin(step)
+                message(peer, peer, FIRST, MSG - FIRST, bsend, brecv).wait_recv()
+
+        for i in range(X_CHIPS):
+            advance(origin(turn * X_CHIPS + i))
+        return carry
+
+    lax.fori_loop(0, Z_CHIPS, take_rest, 0)
 
     def sent(step, carry):
         peer = target(step)
@@ -348,23 +392,36 @@
     return tiles.reshape(COLS, 2, 4, NZ).transpose(0, 2, 1, 3).reshape(shape)
 
 
+def finish(cin, tin, sin, cout, tout, sout, sem):
+    copies = [
+        pltpu.make_async_copy(src, dst, sem.at[i])
+        for i, (src, dst) in enumerate(((tin, tout), (sin, sout), (cin, cout)))
+    ]
+    for copy in copies:
+        copy.start()
+    for copy in copies:
+        copy.wait()
+
+
 def local(coarse_temp, coarse_cond, routes, track_start, track_depth, power, fine_temp, fine_strain):
-    par = jnp.stack(
-        [v.reshape(ROWS).astype(F32) for v in (power, track_start, track_depth, routes)]
-        + [jnp.zeros((ROWS,), F32)] * 4
-    )
+    hbm = pl.BlockSpec(memory_space=pltpu.HBM)
+    dma = pltpu.SemaphoreType.DMA
+    shapes = ((BX, BY, NZ), (COLS * 8, NZ), (COLS * 8, NZ))
     vmem = pl.BlockSpec(memory_space=pltpu.VMEM)
-    dma = pltpu.SemaphoreType.DMA
-    cnew, tout, sout = pl.pallas_call(
+    held = pl.pallas_call(
         kernel,
-        out_shape=(
-            jax.ShapeDtypeStruct((BX, BY, NZ), F32),
-            jax.ShapeDtypeStruct((COLS * 8, NZ), F32),
-            jax.ShapeDtypeStruct((COLS * 8, NZ), F32),
-        ),
-        in_specs=[vmem] * 5,
+        out_shape=tuple(pltpu.VMEM(shape, F32) for shape in shapes),
+        in_specs=[hbm] * 8,
         out_specs=(vmem,) * 3,
         scratch_shapes=[
+            pltpu.VMEM((BX, BY), F32),
+            pltpu.VMEM((BX, BY), jnp.int32),
+            pltpu.VMEM((BX, BY), jnp.int32),
+            pltpu.VMEM((BX, 1, BY), jnp.int32),
+            pltpu.VMEM((BX, BY, NZ), F32),
+            pltpu.VMEM((BX, BY, NZ), F32),
+            pltpu.VMEM((COLS * 8, NZ), F32),
+            pltpu.VMEM((COLS * 8, NZ), F32),
             pltpu.VMEM((DEVS * MSG, NZ), F32),
             pltpu.VMEM((DEVS, MSG, NZ), F32),
             pltpu.VMEM((2, 24, NZ), F32),
@@ -385,12 +442,35 @@
             dma((DEVS,)),
             dma((DEVS,)),
             dma,
+            dma((8,)),
         ],
         compiler_params=pltpu.CompilerParams(
-            collective_id=1, has_side_effects=True, vmem_limit_bytes=40 * 2**20
+            collective_id=1, has_side_effects=True, vmem_limit_bytes=VMEM_BYTES
         ),
         name="amr_step",
-    )(par, coarse_temp, coarse_cond, to_tiles(fine_temp), to_tiles(fine_strain))
+    )(
+        *(
+            pltpu.with_memory_space_constraint(value, pltpu.HBM)
+            for value in (
+                power.reshape(BX, BY),
+                track_start.reshape(BX, BY),
+                track_depth.reshape(BX, BY),
+                routes.reshape(BX, 1, BY),
+                coarse_temp,
+                coarse_cond,
+                to_tiles(fine_temp),
+                to_tiles(fine_strain),
+            )
+        )
+    )
+    cnew, tout, sout = pl.pallas_call(
+        finish,
+        out_shape=tuple(pltpu.HBM(shape, F32) for shape in shapes),
+        in_specs=[vmem] * 3,
+        out_specs=(hbm,) * 3,
+        scratch_shapes=[dma((3,))],
+        name="write_results",
+    )(*(pltpu.with_memory_space_constraint(value, pltpu.VMEM) for value in held))
     return cnew, from_tiles(tout, fine_temp.shape), from_tiles(sout, fine_strain.shape)
 
 

time: 51.1 us -> 41.3 us (0.81)
  the two profiles are of different devices: /device:TPU:92 before, /device:TPU:217 now
where the time goes in v2:
time: 41.3 us; the launch traced here: 41.2 us
  Pallas kernels  40.6 us (98%)
  between operations  0.64 us (2%)
    pallas_call x1, Pallas kernels, local(): pl.pallas_call(kernel, out_shape=tuple((pltpu.VMEM(shape, F32) for shape...  39.4 us
    pallas_call x1, Pallas kernels, local(): pl.pallas_call(finish, out_shape=tuple((pltpu.HBM(shape, F32) for shape i...  1.18 us

profile of v2, /device:TPU:217, one launch (start us, length us, event | category | flops | bytes accessed | tf_op | source)
XLA Modules:
  0.0 41.2 jit_solution(15053485234618477359)
XLA Ops:
  0.6 39.4 %amr_step.1 = (f32[8,16,128]{2,1,0:T(8,128)S(1)}, f32[1536,128]{1,0:T(8,128)S(1)}, f32[1536,128]{1,0:T(8,128)S(1)}) custom-call(f32[8,16]{1,0:T(8,128)} %bitcast.28, s32[8,16]{1,0:T(8,128)} %bitcast.29, s32[8,16]{1,0:T(8,128)} %bitcast.30, s32[8,1,16]{2,1,0:T(1,128)} %bitcast.31, f32[8,16,128]{2,1,0:T(8,128)} %ct_in.1, f32[8,16,128]{2,1,0:T(8,128)} %cc_in.1, ...), custom_call_target="tpu_custom_call" | custom-call | tf_op jit(solution)/shard_map/amr_step/pallas_call | solution.py:411
  40.0 1.2 %write_results.1 = (f32[8,16,128]{2,1,0:T(8,128)}, f32[1536,128]{1,0:T(8,128)}, f32[1536,128]{1,0:T(8,128)}) custom-call(f32[8,16,128]{2,1,0:T(8,128)S(1)} %get-tuple-element.9.cin, f32[1536,128]{1,0:T(8,128)S(1)} %get-tuple-element.10.tin, f32[1536,128]{1,0:T(8,128)S(1)} %get-tuple-element.11.sin), custom_call_target="tpu_custom_call" | custom-call | tf_op jit(solution)/shard_map/write_results/pallas_call | solution.py:466

commit v3 on v2

--- a/solution.py
+++ b/solution.py
@@ -197,7 +197,16 @@
         message(target(step), dev, 0, FIRST, asend, arecv).start()
         return carry
 
-    lax.fori_loop(1, DEVS, send_first, 0)
+    def first_by_turn(i, carry):
+        peer = (dx + i) % X_CHIPS * Z_CHIPS + turn_of(i // X_CHIPS)
+
+        @pl.when(peer != dev)
+        def _():
+            message(peer, dev, 0, FIRST, asend, arecv).start()
+
+        return carry
+
+    lax.fori_loop(0, DEVS, first_by_turn, 0)
     own_first = own(0, FIRST)
     own_first.start()
 
@@ -259,7 +268,8 @@
 
         @pl.when(peer != dev)
         def _():
-            message(peer, dev, FIRST, MSG - FIRST, bsend, brecv).start()
+            message(peer, dev, FIRST, 24, bsend, brecv).start()
+            message(peer, dev, FIRST + 24, 16, bsend, brecv).start()
 
         return carry
 

time: 41.3 us -> 40.9 us (level)
  no operation moved by 1% of the time
where the time goes in v3:
time: 40.9 us; the launch traced here: 40.8 us
  Pallas kernels  40.2 us (98%)
  between operations  0.64 us (2%)
    pallas_call x1, Pallas kernels, local(): pl.pallas_call(kernel, out_shape=tuple((pltpu.VMEM(shape, F32) for shape...  39 us
    pallas_call x1, Pallas kernels, local(): pl.pallas_call(finish, out_shape=tuple((pltpu.HBM(shape, F32) for shape i...  1.18 us

profile of v3, /device:TPU:217, one launch (start us, length us, event | category | flops | bytes accessed | tf_op | source)
XLA Modules:
  0.0 40.8 jit_solution(2628077343479489457)
XLA Ops:
  0.6 39.0 %amr_step.1 = (f32[8,16,128]{2,1,0:T(8,128)S(1)}, f32[1536,128]{1,0:T(8,128)S(1)}, f32[1536,128]{1,0:T(8,128)S(1)}) custom-call(f32[8,16]{1,0:T(8,128)} %bitcast.28, s32[8,16]{1,0:T(8,128)} %bitcast.29, s32[8,16]{1,0:T(8,128)} %bitcast.30, s32[8,1,16]{2,1,0:T(1,128)} %bitcast.31, f32[8,16,128]{2,1,0:T(8,128)} %ct_in.1, f32[8,16,128]{2,1,0:T(8,128)} %cc_in.1, ...), custom_call_target="tpu_custom_call" | custom-call | tf_op jit(solution)/shard_map/amr_step/pallas_call | solution.py:421
  39.6 1.2 %write_results.1 = (f32[8,16,128]{2,1,0:T(8,128)}, f32[1536,128]{1,0:T(8,128)}, f32[1536,128]{1,0:T(8,128)}) custom-call(f32[8,16,128]{2,1,0:T(8,128)S(1)} %get-tuple-element.9.cin, f32[1536,128]{1,0:T(8,128)S(1)} %get-tuple-element.10.tin, f32[1536,128]{1,0:T(8,128)S(1)} %get-tuple-element.11.sin), custom_call_target="tpu_custom_call" | custom-call | tf_op jit(solution)/shard_map/write_results/pallas_call | solution.py:476

commit v4 on v3

--- a/solution.py
+++ b/solution.py
@@ -369,16 +369,16 @@
     loads[7].wait()
 
     def take_rest(turn, carry):
-        for i in range(X_CHIPS):
-            step = turn * X_CHIPS + i
-
-            @pl.when(step > 0)
+        z = turn_of(turn)
+        for x in range(X_CHIPS):
+            peer = x * Z_CHIPS + z
+
+            @pl.when(peer != dev)
             def _():
-                peer = origin(step)
                 message(peer, peer, FIRST, MSG - FIRST, bsend, brecv).wait_recv()
 
-        for i in range(X_CHIPS):
-            advance(origin(turn * X_CHIPS + i))
+        for x in range(X_CHIPS):
+            advance(x * Z_CHIPS + z)
         return carry
 
     lax.fori_loop(0, Z_CHIPS, take_rest, 0)

time: 40.9 us -> 40.5 us (level)
  the two profiles are of different devices: /device:TPU:217 before, /device:TPU:286 now
where the time goes in v4:
time: 40.5 us; the launch traced here: 40.4 us
  Pallas kernels  39.7 us (98%)
  between operations  0.64 us (2%)
    pallas_call x1, Pallas kernels, local(): pl.pallas_call(kernel, out_shape=tuple((pltpu.VMEM(shape, F32) for shape...  38.6 us
    pallas_call x1, Pallas kernels, local(): pl.pallas_call(finish, out_shape=tuple((pltpu.HBM(shape, F32) for shape i...  1.18 us

profile of v4, /device:TPU:286, one launch (start us, length us, event | category | flops | bytes accessed | tf_op | source)
XLA Modules:
  0.0 40.4 jit_solution(9112559057240334481)
XLA Ops:
  0.6 38.6 %amr_step.1 = (f32[8,16,128]{2,1,0:T(8,128)S(1)}, f32[1536,128]{1,0:T(8,128)S(1)}, f32[1536,128]{1,0:T(8,128)S(1)}) custom-call(f32[8,16]{1,0:T(8,128)} %bitcast.28, s32[8,16]{1,0:T(8,128)} %bitcast.29, s32[8,16]{1,0:T(8,128)} %bitcast.30, s32[8,1,16]{2,1,0:T(1,128)} %bitcast.31, f32[8,16,128]{2,1,0:T(8,128)} %ct_in.1, f32[8,16,128]{2,1,0:T(8,128)} %cc_in.1, ...), custom_call_target="tpu_custom_call" | custom-call | tf_op jit(solution)/shard_map/amr_step/pallas_call | solution.py:421
  39.2 1.2 %write_results.1 = (f32[8,16,128]{2,1,0:T(8,128)}, f32[1536,128]{1,0:T(8,128)}, f32[1536,128]{1,0:T(8,128)}) custom-call(f32[8,16,128]{2,1,0:T(8,128)S(1)} %get-tuple-element.9.cin, f32[1536,128]{1,0:T(8,128)S(1)} %get-tuple-element.10.tin, f32[1536,128]{1,0:T(8,128)S(1)} %get-tuple-element.11.sin), custom_call_target="tpu_custom_call" | custom-call | tf_op jit(solution)/shard_map/write_results/pallas_call | solution.py:476
